TPU v7x, 128 devices: a whole 4x4x4 slice. The times are simulated.
128 devices in a mesh: gr: 8 (over y_hi, z), gc: 16 (over y_lo, x, core).
Axes of the slice: x: 4, y: 4 (y_hi: 2, y_lo: 2; y = y_hi * 2 + y_lo), z: 4, core: 2. Of those that a mesh axis runs over, the one named last changes fastest.
Arguments:
- student: bfloat16 [16384, 1024], P(('gr', 'gc')), may hold values from -500 to 500
- teacher: bfloat16 [16384, 1024], P(('gr', 'gc')), may hold values from -500 to 500
Outputs:
- student_grad: float32 [16384, 1024], P(('gr', 'gc'))
All inputs are finite; a program needn't handle non-finite values.
Results may differ from a plain program's by a relative error of at most 0.0085.
Values may be sent and summed in bfloat16 or wider, within the bound.
A program may use at most 64 MiB of HBM per device.

v0:
```python
import jax
import jax.numpy as jnp
from jax import lax
from jax.sharding import PartitionSpec as P

D = 1024


def unit_rows(embedded):
    values = embedded.astype(jnp.float32)
    inverse_rms = lax.rsqrt(jnp.mean(values * values, axis=-1, keepdims=True) + 1e-06)
    unit = (values * inverse_rms * D ** (-0.5)).astype(jnp.bfloat16)
    return (unit, inverse_rms)


def mismatch_of(piece_s, piece_t, other_s, other_t):
    sim_student = lax.dot_general(
        piece_s, other_s, (((1,), (1,)), ((), ())), preferred_element_type=jnp.float32
    )
    sim_teacher = lax.dot_general(
        piece_t, other_t, (((1,), (1,)), ((), ())), preferred_element_type=jnp.float32
    )
    stretch = 0.5 * D**0.5
    return jnp.tanh(stretch * (sim_student - sim_teacher)).astype(jnp.bfloat16)


def local(student, teacher):
    unit_s, inv_s = unit_rows(student)
    unit_t, inv_t = unit_rows(teacher)
    column_s, column_t = (
        lax.all_gather(unit_s, "gr", axis=0, tiled=True),
        lax.all_gather(unit_t, "gr", axis=0, tiled=True),
    )
    row_s, row_t = (
        lax.all_gather(unit_s, "gc", axis=0, tiled=True),
        lax.all_gather(unit_t, "gc", axis=0, tiled=True),
    )
    mismatch = mismatch_of(row_s, row_t, column_s, column_t)
    pull = lax.psum_scatter(
        jnp.dot(mismatch, column_s, preferred_element_type=jnp.float32),
        "gc",
        scatter_dimension=0,
        tiled=True,
    )
    unit_float = unit_s.astype(jnp.float32)
    radial = jnp.sum(unit_float * pull, axis=-1, keepdims=True)
    total_rows = unit_s.shape[0] * lax.axis_size("gr") * lax.axis_size("gc")
    factor = 12.0 * (D / total_rows) ** 0.5
    return factor * inv_s * (pull - radial * unit_float)


def solution(mesh):
    in_specs = (P(("gr", "gc"), None), P(("gr", "gc"), None))
    out_specs = P(("gr", "gc"), None)
    return jax.shard_map(local, mesh=mesh, in_specs=in_specs, out_specs=out_specs, check_vma=False)
```

profile of v0, /device:TPU:0, one launch (start us, length us, event | category | flops | bytes accessed | tf_op | source)
XLA Modules:
  0.0 295.6 jit_solution(11600875809418182227)
XLA Ops:
  6.5 0.0 all-gather.7.cloned.1.call-start
  6.5 1.1 fusion.4
  7.6 1.8 fusion.6
  9.4 0.0 all-gather.7.cloned.1.call-update
  9.4 0.0 all-gather.5.cloned.1.call-start
  9.5 0.7 all-gather.5.cloned.1.call-update
  10.2 0.0 all-gather.11.cloned.1.call-start
  10.2 1.1 fusion.7
  11.3 1.8 fusion.9
  13.1 0.0 all-gather.11.cloned.1.call-update
  13.2 0.0 all-gather.9.cloned.1.call-start
  13.2 0.5 all-gather.9.cloned.1.call-update
  13.7 0.0 reduce-scatter.2.cloned.1.call-start
  13.8 52.6 %all-gather.7.cloned.1.call-done = bf16[1024,1024]{1,0:T(8,128)(2,1)} async-done(((bf16[128,1024]{1,0:T(8,128)(2,1)}), bf16[1024,1024]{1,0:T(8,128)(2,1)}) %all-gather.7.cloned.1.call-update) | async-done | bytes 2097168 | tf_op jit(solution)/shard_map/all_gather | solution.py:31
  66.4 0.0 copy-start.1
  66.4 36.8 %all-gather.5.cloned.1.call-done = bf16[2048,1024]{1,0:T(8,128)(2,1)} async-done(((bf16[128,1024]{1,0:T(8,128)(2,1)}), bf16[2048,1024]{1,0:T(8,128)(2,1)}) %all-gather.5.cloned.1.call-update) | async-done | bytes 4194320 | tf_op jit(solution)/shard_map/all_gather | solution.py:35
  103.2 10.7 %fusion.14 = f32[2048,1024]{1,0:T(8,128)} fusion(bf16[2048,1024]{1,0:T(8,128)(2,1)} %all-gather.5.cloned.1.call-done, bf16[1024,1024]{1,0:T(8,128)(2,1)} %all-gather.7.cloned.1.call-done), kind=kOutput, calls=%fused_computation.23 | convolution fusion | flops 4294967296 | bytes 14680064 | tf_op jit(solution)/shard_map/dot_general | solution.py:17
  113.8 46.0 %all-gather.11.cloned.1.call-done = bf16[1024,1024]{1,0:T(8,128)(2,1)} async-done(((bf16[128,1024]{1,0:T(8,128)(2,1)}), bf16[1024,1024]{1,0:T(8,128)(2,1)}) %all-gather.11.cloned.1.call-update) | async-done | bytes 2097168 | tf_op jit(solution)/shard_map/all_gather | solution.py:32
  159.8 36.6 %all-gather.9.cloned.1.call-done = bf16[2048,1024]{1,0:T(8,128)(2,1)} async-done(((bf16[128,1024]{1,0:T(8,128)(2,1)}), bf16[2048,1024]{1,0:T(8,128)(2,1)}) %all-gather.9.cloned.1.call-update) | async-done | bytes 4194320 | tf_op jit(solution)/shard_map/all_gather | solution.py:36
  196.4 0.0 copy-done.1
  196.4 14.5 %fusion = f32[2048,1024]{1,0:T(8,128)} fusion(bf16[1024,1024]{1,0:T(8,128)(2,1)S(1)} %copy-done.1, f32[2048,1024]{1,0:T(8,128)} %fusion.14, bf16[2048,1024]{1,0:T(8,128)(2,1)} %all-gather.9.cloned.1.call-done, bf16[1024,1024]{1,0:T(8,128)(2,1)} %all-gather.11.cloned.1.call-done), kind=kOutput, calls=%fused_computation.1 | convolution fusion | flops 8596226048 | bytes 25165824 | tf_op jit(solution)/shard_map/dot_general | solution.py:40
  210.9 0.0 copy-start
  210.9 0.0 reduce-scatter.2.cloned.1.call-update
  211.0 74.8 %reduce-scatter.2.cloned.1.call-done = f32[128,1024]{1,0:T(8,128)} async-done(((f32[2048,1024]{1,0:T(8,128)}), f32[128,1024]{1,0:T(8,128)}) %reduce-scatter.2.cloned.1.call-update) | async-done | bytes 524304 | tf_op jit(solution)/shard_map/reduce_scatter | solution.py:39
  285.8 0.0 copy-done
  285.8 1.3 fusion.10
  287.0 2.1 fusion.12
  (2 shorter events, 0.0 us)
Async XLA Ops:
  6.5 59.8 %all-gather.7.cloned.1.call-start = ((), (), s32[]{:S(2)}) async-start(), calls=%async_computation.2 | async-start | bytes 2359296 | tf_op jit(solution)/shard_map/all_gather | solution.py:31
  9.4 93.7 %all-gather.5.cloned.1.call-start = ((), (), s32[]{:S(2)}) async-start(), calls=%async_computation.1 | async-start | bytes 4456448 | tf_op jit(solution)/shard_map/all_gather | solution.py:35
  10.2 149.6 %all-gather.11.cloned.1.call-start = ((), (), s32[]{:S(2)}) async-start(), calls=%async_computation.4 | async-start | bytes 2359296 | tf_op jit(solution)/shard_map/all_gather | solution.py:32
  13.2 183.2 %all-gather.9.cloned.1.call-start = ((), (), s32[]{:S(2)}) async-start(), calls=%async_computation.3 | async-start | bytes 4456448 | tf_op jit(solution)/shard_map/all_gather | solution.py:36
  13.7 272.0 %reduce-scatter.2.cloned.1.call-start = ((), (), s32[]{:S(2)}) async-start(), calls=%async_computation.5 | async-start | bytes 8912896 | tf_op jit(solution)/shard_map/reduce_scatter | solution.py:39
  66.4 130.0 %copy-start.1 = (bf16[1024,1024]{1,0:T(8,128)(2,1)S(1)}, bf16[1024,1024]{1,0:T(8,128)(2,1)}, u32[]{:S(2)}) copy-start(bf16[1024,1024]{1,0:T(8,128)(2,1)} %all-gather.7.cloned.1.call-done) | copy-start | bytes 6291460
  210.9 74.8 %copy-start = (bf16[128,1024]{1,0:T(8,128)(2,1)S(1)}, bf16[128,1024]{1,0:T(8,128)(2,1)}, u32[]{:S(2)}) copy-start(bf16[128,1024]{1,0:T(8,128)(2,1)} %param.2) | copy-start | bytes 786436
Sparse Core Ops, SparseCore 0:
  9.7 56.6 all-gather.6
  68.1 35.0 all-gather.4
  105.5 54.2 all-gather.10
  161.3 35.0 all-gather.8
  211.1 74.6 reduce-scatter.1
where the time goes:
time: 296 us
  waiting for transfers between devices  248 us (84%)
  matrix products  25.2 us (9%)
  between operations  13.1 us (4%)
  other arithmetic  9.12 us (3%)
    reduce_scatter x1, waiting for transfers between devices, local(): lax.psum_scatter(jnp.dot(mismatch, column_s, preferred_element_type=jnp.f...  74.8 us
    all_gather x1, waiting for transfers between devices, local(): lax.all_gather(unit_s, 'gr', axis=0, tiled=True)  52.6 us
    all_gather x1, waiting for transfers between devices, local(): lax.all_gather(unit_t, 'gr', axis=0, tiled=True)  46 us
    all_gather x1, waiting for transfers between devices, local(): lax.all_gather(unit_s, 'gc', axis=0, tiled=True)  36.8 us
    all_gather x1, waiting for transfers between devices, local(): lax.all_gather(unit_t, 'gc', axis=0, tiled=True)  36.6 us
    dot_general x1, matrix products, local(): jnp.dot(mismatch, column_s, preferred_element_type=jnp.float32)  14.5 us
    dot_general x1, matrix products, mismatch_of(): lax.dot_general(piece_s, other_s, (((1,), (1,)), ((), ())), preferred_ele...  10.7 us
  transfers between devices with their start and end apart: 5, of which 5 were waited for; matrix products, arithmetic and copies ran while one was open for 5% of the time, Pallas kernels for 0%

commit v1 on v0

--- a/solution.py
+++ b/solution.py
@@ -29,7 +29,9 @@
     unit_t, inv_t = unit_rows(teacher)
     column_s, column_t = (
         lax.all_gather(unit_s, "gr", axis=0, tiled=True),
-        lax.all_gather(unit_t, "gr", axis=0, tiled=True),
+        jnp.concatenate(
+            lax.all_to_all(jnp.stack([unit_t] * lax.axis_size("gr")), "gr", 0, 0), axis=0
+        ),
     )
     row_s, row_t = (
         lax.all_gather(unit_s, "gc", axis=0, tiled=True),

time: 296 us -> 260 us (0.88)
  waiting for transfers between devices: 248 us -> 201 us
  starting transfers between devices: 0.16 us -> 8.15 us
    all_gather x1 -> x0, waiting for transfers between devices: 46 us -> none  [local(): lax.all_gather(unit_t, 'gr', axis=0, tiled=True)]
    all_gather x1, waiting for transfers between devices: 36.6 us -> 28.5 us  [local(): lax.all_gather(unit_t, 'gc', axis=0, tiled=True)]
    all_to_all x0 -> x1, starting transfers between devices: none -> 8.03 us  [local(): lax.all_to_all(jnp.stack([unit_t] * lax.axis_size('gr')), 'gr', 0, 0)]
    all_gather x1, waiting for transfers between devices: 52.6 us -> 60.2 us  [local(): lax.all_gather(unit_s, 'gr', axis=0, tiled=True)]
  transfers between devices with their start and end apart: 5 -> 5, of which waited for: 5 -> 4; matrix products, arithmetic and copies ran while one was open for 5% -> 6% of each run, Pallas kernels for 0% -> 0%
where the time goes in v1:
time: 260 us; the launch traced here: 259 us
  waiting for transfers between devices  201 us (77%)
  matrix products  25.1 us (10%)
  between operations  13.1 us (5%)
  other arithmetic  9.13 us (4%)
  starting transfers between devices  8.15 us (3%)
    reduce_scatter x1, waiting for transfers between devices, local(): lax.psum_scatter(jnp.dot(mismatch, column_s, preferred_element_type=jnp.f...  74.8 us
    all_gather x1, waiting for transfers between devices, local(): lax.all_gather(unit_s, 'gr', axis=0, tiled=True)  60.2 us
    all_gather x1, waiting for transfers between devices, local(): lax.all_gather(unit_s, 'gc', axis=0, tiled=True)  36.8 us
    all_gather x1, waiting for transfers between devices, local(): lax.all_gather(unit_t, 'gc', axis=0, tiled=True)  28.5 us
    dot_general x1, matrix products, local(): jnp.dot(mismatch, column_s, preferred_element_type=jnp.float32)  14.5 us
    dot_general x1, matrix products, mismatch_of(): lax.dot_general(piece_s, other_s, (((1,), (1,)), ((), ())), preferred_ele...  10.6 us
    all_to_all x1, starting transfers between devices, local(): lax.all_to_all(jnp.stack([unit_t] * lax.axis_size('gr')), 'gr', 0, 0)  8.03 us
  transfers between devices with their start and end apart: 5, of which 4 were waited for; matrix products, arithmetic and copies ran while one was open for 6% of the time, Pallas kernels for 0%

profile of v1, /device:TPU:0, one launch (start us, length us, event | category | flops | bytes accessed | tf_op | source)
XLA Modules:
  0.0 259.1 jit_solution(3167579015269272121)
XLA Ops:
  6.5 0.0 all-gather.6.cloned.1.call-start
  6.5 1.1 fusion.4
  7.6 1.8 fusion.6
  9.4 0.0 all-gather.6.cloned.1.call-update
  9.4 0.0 all-gather.4.cloned.1.call-start
  9.5 0.7 all-gather.4.cloned.1.call-update
  10.2 0.0 all-gather.8.cloned.1.call-start
  10.2 1.1 fusion.7
  11.3 1.8 fusion.9
  13.2 0.0 all-gather.8.cloned.1.call-update
  13.2 2.6 stack.2
  15.7 8.0 %all-to-all-start = ((bf16[8,128,1024]{2,1,0:T(8,128)(2,1)}), bf16[8,128,1024]{2,1,0:T(8,128)(2,1)S(1)}, u32[]{:S(2)}, u32[]{:S(2)}) async-start(bf16[8,128,1024]{2,1,0:T(8,128)(2,1)} %stack.2), calls=%async_computation | async-start | bytes 4194304 | tf_op jit(solution)/shard_map/all_to_all | solution.py:33
  23.8 0.0 reduce-scatter.2.cloned.1.call-start
  23.8 60.2 %all-gather.6.cloned.1.call-done = bf16[1024,1024]{1,0:T(8,128)(2,1)} async-done(((bf16[128,1024]{1,0:T(8,128)(2,1)}), bf16[1024,1024]{1,0:T(8,128)(2,1)}) %all-gather.6.cloned.1.call-update) | async-done | bytes 2097168 | tf_op jit(solution)/shard_map/all_gather | solution.py:31
  84.0 36.8 %all-gather.4.cloned.1.call-done = bf16[2048,1024]{1,0:T(8,128)(2,1)} async-done(((bf16[128,1024]{1,0:T(8,128)(2,1)}), bf16[2048,1024]{1,0:T(8,128)(2,1)}) %all-gather.4.cloned.1.call-update) | async-done | bytes 4194320 | tf_op jit(solution)/shard_map/all_gather | solution.py:37
  120.8 10.6 %fusion.14 = f32[2048,1024]{1,0:T(8,128)} fusion(bf16[2048,1024]{1,0:T(8,128)(2,1)} %all-gather.4.cloned.1.call-done, bf16[1024,1024]{1,0:T(8,128)(2,1)} %all-gather.6.cloned.1.call-done), kind=kOutput, calls=%fused_computation.23 | convolution fusion | flops 4294967296 | bytes 14680064 | tf_op jit(solution)/shard_map/dot_general | solution.py:17
  131.4 0.0 all-to-all-done
  131.4 28.5 %all-gather.8.cloned.1.call-done = bf16[2048,1024]{1,0:T(8,128)(2,1)} async-done(((bf16[128,1024]{1,0:T(8,128)(2,1)}), bf16[2048,1024]{1,0:T(8,128)(2,1)}) %all-gather.8.cloned.1.call-update) | async-done | bytes 4194320 | tf_op jit(solution)/shard_map/all_gather | solution.py:38
  159.9 14.5 %fusion = f32[2048,1024]{1,0:T(8,128)} fusion(bf16[1024,1024]{1,0:T(8,128)(2,1)} %all-gather.6.cloned.1.call-done, f32[2048,1024]{1,0:T(8,128)} %fusion.14, bf16[2048,1024]{1,0:T(8,128)(2,1)} %all-gather.8.cloned.1.call-done, bf16[1024,1024]{1,0:T(8,128)(2,1)S(1)} %bitcast.6), kind=kOutput, calls=%fused_computation.1 | convolution fusion | flops 8596226048 | bytes 25165824 | tf_op jit(solution)/shard_map/dot_general | solution.py:42
  174.4 0.0 copy-start
  174.4 0.0 reduce-scatter.2.cloned.1.call-update
  174.4 74.8 %reduce-scatter.2.cloned.1.call-done = f32[128,1024]{1,0:T(8,128)} async-done(((f32[2048,1024]{1,0:T(8,128)}), f32[128,1024]{1,0:T(8,128)}) %reduce-scatter.2.cloned.1.call-update) | async-done | bytes 524304 | tf_op jit(solution)/shard_map/reduce_scatter | solution.py:41
  249.2 0.0 copy-done
  249.2 1.3 fusion.10
  250.5 2.1 fusion.12
  (2 shorter events, 0.0 us)
Async XLA Ops:
  6.5 77.4 %all-gather.6.cloned.1.call-start = ((), (), s32[]{:S(2)}) async-start(), calls=%async_computation.3 | async-start | bytes 2359296 | tf_op jit(solution)/shard_map/all_gather | solution.py:31
  9.4 111.3 %all-gather.4.cloned.1.call-start = ((), (), s32[]{:S(2)}) async-start(), calls=%async_computation.2 | async-start | bytes 4456448 | tf_op jit(solution)/shard_map/all_gather | solution.py:37
  10.2 149.7 %all-gather.8.cloned.1.call-start = ((), (), s32[]{:S(2)}) async-start(), calls=%async_computation.4 | async-start | bytes 4456448 | tf_op jit(solution)/shard_map/all_gather | solution.py:38
  15.7 115.7 %all-to-all-start = ((bf16[8,128,1024]{2,1,0:T(8,128)(2,1)}), bf16[8,128,1024]{2,1,0:T(8,128)(2,1)S(1)}, u32[]{:S(2)}, u32[]{:S(2)}) async-start(bf16[8,128,1024]{2,1,0:T(8,128)(2,1)} %stack.2), calls=%async_computation | async-start | bytes 4194304 | tf_op jit(solution)/shard_map/all_to_all | solution.py:33
  23.8 225.4 %reduce-scatter.2.cloned.1.call-start = ((), (), s32[]{:S(2)}) async-start(), calls=%async_computation.5 | async-start | bytes 8912896 | tf_op jit(solution)/shard_map/reduce_scatter | solution.py:41
  174.4 74.8 %copy-start = (bf16[128,1024]{1,0:T(8,128)(2,1)S(1)}, bf16[128,1024]{1,0:T(8,128)(2,1)}, u32[]{:S(2)}) copy-start(bf16[128,1024]{1,0:T(8,128)(2,1)} %param.2) | copy-start | bytes 786436
Sparse Core Ops, SparseCore 0:
  9.7 74.2 all-gather.5
  85.7 35.0 all-gather.3
  122.5 37.3 all-gather.7
  174.5 74.6 reduce-scatter.1
